TPU v7x, 32 devices: a whole 2x2x4 slice. The times are simulated.
32 devices in a mesh: tm: 4 (over z), height: 8 (over y, x, core).
Axes of the slice: x: 2, y: 2, z: 4, core: 2. Of those that a mesh axis runs over, the one named last changes fastest.
Arguments:
- queries: bfloat16 [8, 8, 160, 2560], P('tm', 'height'), may hold values from -6 to 6
- keys: bfloat16 [8, 8, 160, 2560], P('tm', 'height'), may hold values from -6 to 6
- values: bfloat16 [8, 8, 160, 2560], P('tm', 'height'), may hold values from -6 to 6
- head_window_radius: int32 [20, 3], replicated, may hold values from 0 to 2, as said below
- output_weight: bfloat16 [2560, 2560], P('height'), may hold values from -0.125 to 0.125
- adapter_down_weight: bfloat16 [2560, 64], replicated, may hold values from -0.125 to 0.125
- adapter_up_weight: bfloat16 [64, 2560], replicated, may hold values from -0.75 to 0.75
- output_gradient: bfloat16 [8, 8, 160, 2560], P('tm', 'height'), may hold values from -6 to 6
Outputs:
- mixed: bfloat16 [8, 8, 160, 2560], P('tm', 'height')
- attention_gradient: bfloat16 [8, 8, 160, 2560], P('tm', 'height')
- grad_up: float32 [64, 2560], replicated
- grad_down: float32 [2560, 64], replicated
Inputs may be any that keep to these rules, and one draw needn't show every extreme that they name: `head_window_radius`: radii along frames and rows are 0 or 1, along columns 0 to 2; along each axis some head has the largest radius.
All inputs are finite; a program needn't handle non-finite values.
Results may differ from a plain program's by a relative error of at most 0.0063.
Values may be sent and summed in bfloat16 or wider, within the bound.
No kernel may reach another device: no remote copies, remote signals or barrier semaphores. Data moves between devices by JAX's collectives and lax.ppermute only.
A program may use at most 128 MiB of HBM per device.

v0:
```python
import math

import jax
import jax.numpy as jnp
from jax import lax
from jax.sharding import PartitionSpec as P

HEADS = 20
HEAD_DIM = 128
TILE_W = 16


ADAPTER_SCALE = 2.0


def with_halo(cells, sides, width):
    for axis, dim in sides:
        count = lax.axis_size(axis)
        ends = count - 1
        head = lax.slice_in_dim(cells, 0, width, axis=dim)
        tail = lax.slice_in_dim(cells, cells.shape[dim] - width, cells.shape[dim], axis=dim)
        cells = jnp.concatenate(
            [
                lax.ppermute(tail, axis, [(i, (i + 1) % count) for i in range(ends)]),
                cells,
                lax.ppermute(head, axis, [((i + 1) % count, i) for i in range(ends)]),
            ],
            axis=dim,
        )
    return cells


def per_device(
    queries,
    keys,
    values,
    head_window_radius,
    output_weight,
    adapter_down_weight,
    adapter_up_weight,
    output_gradient,
):
    frames, row_total, column_count, feature_width = queries.shape
    out_width = output_gradient.shape[3]
    key_value = jnp.stack([keys, values])
    extended = with_halo(key_value, (("tm", 1), ("height", 2)), 1)
    frame_base = lax.axis_index("tm") * frames
    row_base = lax.axis_index("height") * row_total
    all_frames = frames * lax.axis_size("tm")
    all_rows = row_total * lax.axis_size("height")
    query_shape = (frames, row_total, column_count)
    key_shape = (frames + 2, row_total + 2, column_count)
    query_frame = jnp.broadcast_to(
        (frame_base + jnp.arange(frames, dtype=jnp.int32))[:, None, None], query_shape
    ).reshape(-1)
    query_row = jnp.broadcast_to(
        (row_base + jnp.arange(row_total, dtype=jnp.int32))[None, :, None], query_shape
    ).reshape(-1)
    query_tile = jnp.broadcast_to(
        (jnp.arange(column_count, dtype=jnp.int32) // TILE_W)[None, None, :], query_shape
    ).reshape(-1)
    key_frame = jnp.broadcast_to(
        (frame_base - 1 + jnp.arange(frames + 2, dtype=jnp.int32))[:, None, None], key_shape
    ).reshape(-1)
    key_row = jnp.broadcast_to(
        (row_base - 1 + jnp.arange(row_total + 2, dtype=jnp.int32))[None, :, None], key_shape
    ).reshape(-1)
    key_tile = jnp.broadcast_to(
        (jnp.arange(column_count, dtype=jnp.int32) // TILE_W)[None, None, :], key_shape
    ).reshape(-1)
    valid = (key_frame >= 0) & (key_frame < all_frames) & (key_row >= 0) & (key_row < all_rows)
    far_away = 1 << 20
    diff_frame = jnp.where(
        valid[None, :], jnp.abs(query_frame[:, None] - key_frame[None, :]), far_away
    )
    diff_row = jnp.abs(query_row[:, None] - key_row[None, :])
    diff_tile = jnp.abs(query_tile[:, None] - key_tile[None, :])
    token_count = frames * row_total * column_count
    query_flat = queries.reshape(token_count, feature_width)
    key_flat = extended[0].reshape(-1, feature_width)
    value_flat = extended[1].reshape(-1, feature_width)

    def one_head(head_index, attention_output):
        offset_first = head_index * HEAD_DIM
        query_head = lax.dynamic_slice_in_dim(query_flat, offset_first, HEAD_DIM, 1)
        key_head = lax.dynamic_slice_in_dim(key_flat, offset_first, HEAD_DIM, 1)
        value_head = lax.dynamic_slice_in_dim(value_flat, offset_first, HEAD_DIM, 1)
        scores = lax.dot_general(
            query_head, key_head, (((1,), (1,)), ((), ())), preferred_element_type=jnp.float32
        ) / math.sqrt(HEAD_DIM)
        radius = lax.dynamic_index_in_dim(head_window_radius, head_index, 0, keepdims=False)
        allowed = (diff_frame <= radius[0]) & (diff_row <= radius[1]) & (diff_tile <= radius[2])
        scores = jnp.where(allowed, scores, -1e30)
        highest = jnp.max(scores, axis=-1, keepdims=True)
        weights = jnp.exp(scores - highest)
        weights = (weights / jnp.sum(weights, axis=-1, keepdims=True)).astype(jnp.bfloat16)
        result = jnp.dot(weights, value_head, preferred_element_type=jnp.float32).astype(
            jnp.bfloat16
        )
        return lax.dynamic_update_slice_in_dim(attention_output, result, offset_first, 1)

    attention_output = lax.fori_loop(
        0, HEADS, one_head, jnp.zeros((token_count, feature_width), jnp.bfloat16)
    )
    output_cotangent = output_gradient.reshape(token_count, out_width)
    frozen_product = jnp.dot(
        attention_output,
        lax.all_gather(output_weight, "height", axis=0, tiled=True),
        preferred_element_type=jnp.float32,
    )
    frozen_backward = lax.dot_general(
        output_cotangent,
        lax.all_gather(output_weight, "height", axis=0, tiled=True),
        (((1,), (1,)), ((), ())),
        preferred_element_type=jnp.float32,
    )
    low_rank_product = jnp.dot(
        attention_output, adapter_down_weight, preferred_element_type=jnp.float32
    ).astype(jnp.bfloat16)
    mixed = frozen_product + ADAPTER_SCALE * jnp.dot(
        low_rank_product, adapter_up_weight, preferred_element_type=jnp.float32
    )
    low_rank_backward = lax.dot_general(
        output_cotangent,
        adapter_up_weight,
        (((1,), (1,)), ((), ())),
        preferred_element_type=jnp.float32,
    ).astype(jnp.bfloat16)
    attention_gradient = frozen_backward + ADAPTER_SCALE * lax.dot_general(
        low_rank_backward,
        adapter_down_weight,
        (((1,), (1,)), ((), ())),
        preferred_element_type=jnp.float32,
    )
    token_total = token_count * lax.axis_size("tm") * lax.axis_size("height")
    adapter_factor = ADAPTER_SCALE / math.sqrt(token_total)
    local_up = adapter_factor * lax.dot_general(
        low_rank_product,
        output_cotangent,
        (((0,), (0,)), ((), ())),
        preferred_element_type=jnp.float32,
    )
    local_down = adapter_factor * lax.dot_general(
        attention_output,
        low_rank_backward,
        (((0,), (0,)), ((), ())),
        preferred_element_type=jnp.float32,
    )
    grad_up, grad_down = lax.psum((local_up, local_down), ("tm", "height"))
    mixed = mixed.astype(jnp.bfloat16).reshape(frames, row_total, column_count, out_width)
    attention_gradient = attention_gradient.astype(jnp.bfloat16).reshape(
        frames, row_total, column_count, feature_width
    )
    return (mixed, attention_gradient, grad_up, grad_down)


def solution(mesh):
    in_specs = (
        P("tm", "height", None, None),
        P("tm", "height", None, None),
        P("tm", "height", None, None),
        P(),
        P("height", None),
        P(),
        P(),
        P("tm", "height", None, None),
    )
    out_specs = (P("tm", "height", None, None), P("tm", "height", None, None), P(), P())
    return jax.shard_map(
        per_device, mesh=mesh, in_specs=in_specs, out_specs=out_specs, check_vma=False
    )
```

profile of v0, /device:TPU:0, one launch (start us, length us, event | category | flops | bytes accessed | tf_op | source)
XLA Modules:
  0.0 587.0 jit_solution(5609924602421514868)
XLA Ops:
  10.4 5.2 collective-permute-start
  16.9 33.6 %collective-permute-done = bf16[2,1,1,160,2560]{4,3,1,2,0:T(8,128)(2,1)S(1)} collective-permute-done((bf16[2,1,1,160,2560]{4,3,1,2,0:T(8,128)(2,1)S(1)}, bf16[2,1,1,160,2560]{4,3,1,2,0:T(8,128)(2,1)S(1)}, u32[]{:S(2)}, u32[]{:S(2)}) %collective-permute-start) | collective-permute-done | bytes 1638432 | tf_op jit(solution)/shard_map/ppermute | solution.py:24
  50.5 4.2 collective-permute-done.1
  70.0 5.0 collective-permute-done.3
  75.0 9.5 %pad_maximum_fusion = bf16[2,4,3,160,2560]{4,3,1,2,0:T(8,128)(2,1)S(1)} fusion(bf16[2,4,1,160,2560]{4,3,1,2,0:T(8,128)(2,1)} %collective-permute-done.3, bf16[2,1,1,160,2560]{4,3,1,2,0:T(8,128)(2,1)} %copy-done.5, bf16[1,2,1,160,2560]{4,3,1,2,0:T(8,128)(2,1)S(1)} %bitcast.45, bf16[1,2,1,160,2560]{4,3,1,2,0:T(8,128)(2,1)S(1)} %bitcast.42, ...), kind=kLoop, calls=%fused_computation.22 | loop fusion | flops 49152000 | bytes 39321600 | tf_op jit(solution)/shard_map/concatenate | solution.py:22
  84.5 6.9 %fusion.27 = (bf16[1,4,3,160,2560]{4,3,1,2,0:T(8,128)(2,1)}, bf16[1,4,3,160,2560]{4,3,1,2,0:T(8,128)(2,1)}) fusion(bf16[2,4,3,160,2560]{4,3,1,2,0:T(8,128)(2,1)S(1)} %pad_maximum_fusion), kind=kLoop, calls=%fused_computation.53 | loop fusion | bytes 39321600 | tf_op jit(solution)/shard_map/slice | solution.py:81
  91.4 8.1 %copy.16 = bf16[1,4,3,160,2560]{4,3,2,1,0:T(8,128)(2,1)} copy(bf16[1,4,3,160,2560]{4,3,1,2,0:T(8,128)(2,1)} %get-tuple-element.233) | data formatting | bytes 19660800 | tf_op jit(solution)/shard_map/slice | solution.py:80
  99.6 8.1 %copy.17 = bf16[1,4,3,160,2560]{4,3,2,1,0:T(8,128)(2,1)} copy(bf16[1,4,3,160,2560]{4,3,1,2,0:T(8,128)(2,1)} %get-tuple-element.232) | data formatting | bytes 19660800 | tf_op jit(solution)/shard_map/slice | solution.py:81
  107.8 151.7 %while.14 = (s32[]{:T(128)}, bf16[320,2560]{1,0:T(8,128)(2,1)S(1)}, s32[20,3]{0,1:T(4,128)S(1)}, bf16[320,2560]{1,0:T(8,128)(2,1)}, bf16[1920,2560]{1,0:T(8,128)...) while((s32[]{:T(128)}, bf16[320,2560]{1,0:T(8,128)(2,1)S(1)}, ...), condition=%wide.region_3.4_spmd.clone, body=%wide.region_0.3_spmd.clone.sunk | while | flops 325059840 | bytes 8562299 | solution.py:102
  109.1 4.1 fusion.53
  116.7 4.4 fusion.53
  124.5 4.1 fusion.53
  132.1 4.1 fusion.53
  139.6 4.1 fusion.53
  147.2 4.1 fusion.53
  154.8 4.1 fusion.53
  162.4 4.1 fusion.53
  169.9 4.1 fusion.53
  177.5 4.1 fusion.53
  185.1 4.1 fusion.53
  192.7 4.1 fusion.53
  200.2 4.1 fusion.53
  207.8 4.1 fusion.53
  215.4 4.1 fusion.53
  222.9 4.1 fusion.53
  230.5 4.1 fusion.53
  238.1 4.1 fusion.53
  245.7 4.1 fusion.53
  253.2 4.1 fusion.53
  263.7 7.5 %fusion.28 = f32[320,2560]{1,0:T(8,128)S(1)} fusion(bf16[320,2560]{1,0:T(8,128)(2,1)S(1)} %get-tuple-element.158, bf16[2560,2560]{1,0:T(8,128)(2,1)} %all-gather.2.cloned.1.call-done), kind=kOutput, calls=%fused_computation.54 | convolution fusion | flops 4194304000 | bytes 18022400 | tf_op jit(solution)/shard_map/dot_general | solution.py:106
  271.2 7.6 %fusion.29 = f32[320,2560]{1,0:T(8,128)S(1)} fusion(bf16[320,2560]{1,0:T(8,128)(2,1)S(1)} %bitcast.37, bf16[2560,2560]{1,0:T(8,128)(2,1)} %all-gather.2.cloned.1.call-done), kind=kOutput, calls=%fused_computation.55 | convolution fusion | flops 4194304000 | bytes 18022400 | tf_op jit(solution)/shard_map/dot_general | solution.py:111
  282.4 293.2 %all-reduce.3.cloned.1.call-done = (f32[64,2560]{1,0:T(8,128)}, f32[2560,64]{0,1:T(8,128)}) async-done(((f32[64,2560]{1,0:T(8,128)}, f32[2560,64]{0,1:T(8,128)}), (f32[64,2560]{1,0:T(8,128)}, f32[2560,64]{0,1:T(8,128)})) %all-reduce.3.cloned.1.call-update) | async-done | bytes 1310736 | tf_op jit(solution)/shard_map/psum | solution.py:149
  (158 shorter events, 98.7 us)
Async XLA Ops:
  8.0 56.7 %copy-start = (bf16[2,1,160,2560]{3,2,1,0:T(8,128)(2,1)S(1)}, bf16[2,1,160,2560]{3,2,1,0:T(8,128)(2,1)}, u32[]{:S(2)}) copy-start(bf16[2,1,160,2560]{3,2,1,0:T(8,128)(2,1)} %param.17) | copy-start | bytes 4915204
  8.0 255.7 %all-gather.2.cloned.1.call-start = ((), (), s32[]{:S(2)}) async-start(), calls=%async_computation | async-start | bytes 14745600 | tf_op jit(solution)/shard_map/all_gather | solution.py:108
  8.1 46.7 %copy-start.1 = (bf16[2,1,160,2560]{3,2,1,0:T(8,128)(2,1)S(1)}, bf16[2,1,160,2560]{3,2,1,0:T(8,128)(2,1)}, u32[]{:S(2)}) copy-start(bf16[2,1,160,2560]{3,2,1,0:T(8,128)(2,1)} %param.11) | copy-start | bytes 4915204
  8.1 46.7 %copy-start.2 = (bf16[2,1,160,2560]{3,2,1,0:T(8,128)(2,1)S(1)}, bf16[2,1,160,2560]{3,2,1,0:T(8,128)(2,1)}, u32[]{:S(2)}) copy-start(bf16[2,1,160,2560]{3,2,1,0:T(8,128)(2,1)} %param.12) | copy-start | bytes 4915204
  10.4 40.1 %collective-permute-start = (bf16[2,1,1,160,2560]{4,3,1,2,0:T(8,128)(2,1)S(1)}, bf16[2,1,1,160,2560]{4,3,1,2,0:T(8,128)(2,1)S(1)}, u32[]{:S(2)}, u32[]{:S(2)}) collective-permute-start(bf16[2,1,1,160,2560]{4,3,1,2,0:T(8,128)(2,1)S(1)} %get-tuple-element.234), channel_id=1, source_target_pairs={{0,8},{8,16},{16,24},{1,9},{9,17},{17,25},{2,10},{10,18},{18,26},{... | collective-permute-start | bytes 4915208 | tf_op jit(solution)/shard_map/ppermute | solution.py:24
  15.6 39.2 %collective-permute-start.1 = (bf16[2,1,1,160,2560]{4,3,1,2,0:T(8,128)(2,1)S(1)}, bf16[2,1,1,160,2560]{4,3,1,2,0:T(8,128)(2,1)S(1)}, u32[]{:S(2)}, u32[]{:S(2)}) collective-permute-start(bf16[2,1,1,160,2560]{4,3,1,2,0:T(8,128)(2,1)S(1)} %get-tuple-element.235), channel_id=1, source_target_pairs={{8,0},{16,8},{24,16},{9,1},{17,9},{25,17},{10,2},{18,10},{26,18},{... | collective-permute-start | bytes 4915208 | tf_op jit(solution)/shard_map/ppermute | solution.py:26
  50.5 7.7 %copy-start.4 = (bf16[2,1,1,160,2560]{4,3,1,2,0:T(8,128)(2,1)}, bf16[2,1,1,160,2560]{4,3,1,2,0:T(8,128)(2,1)S(1)}, u32[]{:S(2)}) copy-start(bf16[2,1,1,160,2560]{4,3,1,2,0:T(8,128)(2,1)S(1)} %collective-permute-done) | copy-start | bytes 4915204
  54.7 3.5 copy-start.5
  58.2 11.8 %collective-permute-start.2 = (bf16[2,4,1,160,2560]{4,3,1,2,0:T(8,128)(2,1)}, bf16[2,4,1,160,2560]{4,3,1,2,0:T(8,128)(2,1)}, u32[]{:S(2)}, u32[]{:S(2)}) collective-permute-start(bf16[2,4,1,160,2560]{4,3,1,2,0:T(8,128)(2,1)} %pad_maximum_fusion.1), channel_id=1, source_target_pairs={{0,1},{1,2},{2,3},{3,4},{4,5},{5,6},{6,7},{8,9},{9,10},{10,11},{11... | collective-permute-start | bytes 19660808 | tf_op jit(solution)/shard_map/ppermute | solution.py:24
  62.3 12.8 %collective-permute-start.3 = (bf16[2,4,1,160,2560]{4,3,1,2,0:T(8,128)(2,1)}, bf16[2,4,1,160,2560]{4,3,1,2,0:T(8,128)(2,1)}, u32[]{:S(2)}, u32[]{:S(2)}) collective-permute-start(bf16[2,4,1,160,2560]{4,3,1,2,0:T(8,128)(2,1)} %pad_maximum_fusion.1), channel_id=1, source_target_pairs={{1,0},{2,1},{3,2},{4,3},{5,4},{6,5},{7,6},{9,8},{10,9},{11,10},{12... | collective-permute-start | bytes 19660808 | tf_op jit(solution)/shard_map/ppermute | solution.py:26
  63.6 512.0 %all-reduce.3.cloned.1.call-start = ((), (), s32[]{:S(2)}) async-start(), calls=%async_computation.1 | async-start | bytes 2621440 | tf_op jit(solution)/shard_map/psum | solution.py:149
  64.7 10.3 %copy-start.3 = (bf16[2,1,160,2560]{3,2,1,0:T(8,128)(2,1)S(1)}, bf16[2,1,160,2560]{3,2,1,0:T(8,128)(2,1)}, u32[]{:S(2)}) copy-start(bf16[2,1,160,2560]{3,2,1,0:T(8,128)(2,1)} %param.12) | copy-start | bytes 4915204
  99.6 8.2 %copy-start.8 = (s32[20,3]{0,1:T(4,128)S(1)}, s32[20,3]{0,1:T(4,128)}, u32[]{:S(2)}) copy-start(s32[20,3]{0,1:T(4,128)} %param.13) | copy-start | bytes 724
  271.2 7.6 %copy-start.6 = (bf16[64,2560]{1,0:T(8,128)(2,1)S(1)}, bf16[64,2560]{1,0:T(8,128)(2,1)}, u32[]{:S(2)}) copy-start(bf16[64,2560]{1,0:T(8,128)(2,1)} %param.16) | copy-start | bytes 983044
  278.8 1.8 copy-start.7
Sparse Core Ops, SparseCore 0:
  63.7 127.7 all-gather.1
Sparse Core Ops, SparseCore 1:
  263.8 311.8 all-reduce.2
where the time goes:
time: 589 us; the launch traced here: 587 us
  waiting for transfers between devices  340 us (58%)
  matrix products  140 us (24%)
  local copies, waits for them, and re-layouts  40.2 us (7%)
  other arithmetic  38.3 us (7%)
  between operations  15.7 us (3%)
  starting transfers between devices  11.8 us (2%)
    psum x1, waiting for transfers between devices, per_device(): grad_up, grad_down = lax.psum((local_up, local_down), ('tm', 'height'))  293 us
    dot_general x20, matrix products, one_head(): lax.dot_general(query_head, key_head, (((1,), (1,)), ((), ())), preferred...  82.9 us
    ppermute x2, waiting for transfers between devices, with_halo(): lax.ppermute(tail, axis, [(i, (i + 1) % count) for i in range(ends)])  37.2 us
    dot_general x20, matrix products, one_head(): jnp.dot(weights, value_head, preferred_element_type=jnp.float32)  33.1 us
    slice x2, local copies, waits for them, and re-layouts, per_device(): value_flat = extended[1].reshape(-1, feature_width)  15 us
    concatenate x2, other arithmetic, with_halo(): jnp.concatenate([lax.ppermute(tail, axis, [(i, (i + 1) % count) for i in...  13 us
    le x20, other arithmetic, one_head(): diff_row <= radius[1]  13 us
  transfers between devices with their start and end apart: 6, of which 5 were waited for; matrix products, arithmetic and copies ran while one was open for 36% of the time, Pallas kernels for 0%

commit v1 on v0

v1 whole, which is shorter than its diff:
```python
import functools
import math

import jax
import jax.numpy as jnp
from jax import lax
from jax.experimental import pallas as pl
from jax.experimental.pallas import tpu as pltpu
from jax.sharding import PartitionSpec as P

HEADS = 20
HEAD_DIM = 128
TILE_W = 16
ADAPTER_SCALE = 2.0
MASKED = -1e30
ATTENTION_VMEM = 16 * 1024 * 1024
FAR = 100

TIERS = ((20, 20, 20), (13, 14, 9))

ORDER = 0
COL_RADIUS = HEADS
COUNTS = 2 * HEADS
VALID = COUNTS + 3
TIER = VALID + 3
PLACE = TIER + 1
RELAYED = PLACE + 1
TABLE = RELAYED + 1


def table_kernel(places_ref, radius_ref, table_ref):
    def need_of(head):
        frame, row = radius_ref[0, head], radius_ref[1, head]
        return jnp.where(row > 0, jnp.where(frame > 0, 0, 1), jnp.where(frame > 0, 3, 2))

    def fill(need):
        def step(head, place):
            hit = need_of(head) == need

            @pl.when(hit)
            def _():
                table_ref[ORDER + place] = head
                table_ref[COL_RADIUS + place] = radius_ref[2, head]

            return place + hit.astype(jnp.int32)

        return step

    place = jnp.zeros((), jnp.int32)
    for need in range(4):
        place = lax.fori_loop(0, HEADS, fill(need), place)
        if need < 3:
            table_ref[COUNTS + need] = place
    table_ref[VALID] = (places_ref[0] > 0).astype(jnp.int32)
    table_ref[VALID + 1] = (places_ref[0] < places_ref[1] - 1).astype(jnp.int32)
    last = jnp.where((places_ref[2] & 1) == 1, places_ref[3] - 1, 0)
    table_ref[VALID + 2] = (places_ref[2] != last).astype(jnp.int32)
    first, second, third = (table_ref[COUNTS + i] for i in range(3))
    tier = jnp.zeros((), jnp.int32)
    for row_size, frame_size, corner_size in TIERS[1:]:
        fits = (second <= row_size) & (HEADS - third + first <= frame_size) & (first <= corner_size)
        tier += fits.astype(jnp.int32)
    table_ref[TIER] = tier
    table_ref[PLACE] = places_ref[2]
    table_ref[RELAYED] = ((places_ref[2] == 3) | (places_ref[2] == 4)).astype(jnp.int32)


def head_table(radius):
    places = jnp.stack(
        [
            lax.axis_index("tm"),
            jnp.int32(lax.axis_size("tm")),
            lax.axis_index("height"),
            jnp.int32(lax.axis_size("height")),
        ]
    ).astype(jnp.int32)
    smem = pl.BlockSpec(memory_space=pltpu.SMEM)
    return pl.pallas_call(
        table_kernel,
        in_specs=[smem, smem],
        out_specs=smem,
        out_shape=jax.ShapeDtypeStruct((TABLE,), jnp.int32),
        name="head_table",
    )(places, radius.T)


def head_lanes(table_ref, slot):
    return pl.ds(pl.multiple_of(table_ref[ORDER + slot] * HEAD_DIM, HEAD_DIM), HEAD_DIM)


def pack_rows_kernel(table_ref, keys_ref, values_ref, rows_ref, *part_refs):
    def fill(refs, start, size):
        @pl.loop(0, size)
        def _(i):
            at = head_lanes(table_ref, start + i)
            for frame in range(2):
                key, value = keys_ref[frame, 0, :, at], values_ref[frame, 0, :, at]
                for ref, first in refs:
                    ref[frame, first + i, 0] = key
                    ref[frame, first + i, 1] = value

    start = 0
    for part_ref in part_refs:
        fill([(part_ref, 0), (rows_ref, start)], start, part_ref.shape[1])
        start += part_ref.shape[1]
    if not part_refs:
        fill([(rows_ref, 0)], 0, rows_ref.shape[1])


def pack_edges_kernel(table_ref, keys_ref, values_ref, rows_ref, last_ref, first_ref):
    @pl.loop(0, last_ref.shape[0])
    def _(place):
        first, third = table_ref[COUNTS], table_ref[COUNTS + 2]
        slot = jnp.where(place < first, place, third + place - first)
        at = head_lanes(table_ref, jnp.minimum(slot, HEADS - 1))
        first_ref[place, 0] = keys_ref[0, 0, :, at]
        first_ref[place, 1] = values_ref[0, 0, :, at]
        last_ref[place, 0] = keys_ref[1, 0, :, at]
        last_ref[place, 1] = values_ref[1, 0, :, at]


def pack(table, keys, values, row_size, frame_size, parted):
    frames, rows, columns, width = keys.shape
    smem = pl.BlockSpec(memory_space=pltpu.SMEM)
    vmem = pl.BlockSpec(memory_space=pltpu.VMEM)
    params = pltpu.CompilerParams(vmem_limit_bytes=24 * 1024 * 1024)
    edge = jax.ShapeDtypeStruct((frame_size, 2, columns, HEAD_DIM), keys.dtype)
    rows_of = lambda size: jax.ShapeDtypeStruct(
        (frames, size, 2, columns, HEAD_DIM), keys.dtype
    )
    sizes = [row_size] + ([row_size - row_size // 2, row_size // 2] if parted else [])
    packed = pl.pallas_call(
        pack_rows_kernel,
        in_specs=[smem, vmem, vmem],
        out_specs=[vmem] * len(sizes),
        out_shape=[rows_of(size) for size in sizes],
        compiler_params=params,
        cost_estimate=pl.CostEstimate(flops=0, bytes_accessed=8_000_000, transcendentals=0),
        name="pack_rows",
    )(table, keys, values)
    last, first = pl.pallas_call(
        pack_edges_kernel,
        in_specs=[smem, vmem, vmem, pl.BlockSpec(memory_space=pl.ANY)],
        out_specs=[vmem, vmem],
        out_shape=[edge, edge],
        compiler_params=params,
        cost_estimate=pl.CostEstimate(flops=0, bytes_accessed=6_000_000, transcendentals=0),
        name="pack_edges",
    )(table, keys, values, packed[0])
    return packed, last, first


def cell_distance(columns, cells):
    shape = (columns, cells * columns)
    lane = lax.broadcasted_iota(jnp.int32, shape, 1)
    cell = jnp.zeros(shape, jnp.int32)
    for i in range(1, cells):
        cell += (lane >= i * columns).astype(jnp.int32)
    tile = (lane - cell * columns) >> 4
    query_tile = lax.broadcasted_iota(jnp.int32, shape, 0) >> 4
    return cell, jnp.abs(query_tile - tile)


def bad(flag):
    return jnp.where(flag > 0, 0, FAR)


def masks_kernel(table_ref, row_ref, frame_ref, both_ref, side_ref):
    columns = row_ref.shape[0]
    ok_before, ok_after = table_ref[VALID], table_ref[VALID + 1]
    ok_outer = table_ref[VALID + 2]
    cell, far = cell_distance(columns, 3)
    row_ref[...] = far + jnp.where(cell == 0, bad(ok_outer), 0)
    frame_ref[0] = far + jnp.where(cell == 0, bad(ok_before), 0)
    frame_ref[1] = far + jnp.where(cell == 2, bad(ok_after), 0)
    cell, far = cell_distance(columns, 9)
    frame_cell = (cell >= 3).astype(jnp.int32) + (cell >= 6).astype(jnp.int32)
    far = far + jnp.where(cell - 3 * frame_cell == 0, bad(ok_outer), 0)
    both_ref[0] = far + jnp.where(frame_cell == 0, bad(ok_before), 0)
    both_ref[1] = far + jnp.where(frame_cell == 2, bad(ok_after), 0)
    for bit in range(side_ref.shape[0]):
        side_ref[bit] = jnp.full(side_ref.shape[1:], (table_ref[PLACE] >> bit) & 1, jnp.int32)


def make_masks(table, columns, bits, width):
    vmem = pl.BlockSpec(memory_space=pltpu.VMEM)
    return pl.pallas_call(
        masks_kernel,
        in_specs=[pl.BlockSpec(memory_space=pltpu.SMEM)],
        out_specs=[vmem] * 4,
        out_shape=[
            jax.ShapeDtypeStruct((columns, 3 * columns), jnp.int32),
            jax.ShapeDtypeStruct((2, columns, 3 * columns), jnp.int32),
            jax.ShapeDtypeStruct((2, columns, 9 * columns), jnp.int32),
            jax.ShapeDtypeStruct((bits, 1, width), jnp.int32),
        ],
        compiler_params=pltpu.CompilerParams(vmem_limit_bytes=16 * 1024 * 1024),
        cost_estimate=pl.CostEstimate(flops=0, bytes_accessed=8_000_000, transcendentals=0),
        name="masks",
    )(table)


def attend(query, keys, values, far, radius_col):
    key = jnp.concatenate(keys, axis=0) if len(keys) > 1 else keys[0]
    value = jnp.concatenate(values, axis=0) if len(values) > 1 else values[0]
    scale = math.log2(math.e) / math.sqrt(HEAD_DIM)
    scores = lax.dot_general(
        query, key, (((1,), (1,)), ((), ())), preferred_element_type=jnp.float32
    )
    scores = jnp.where(far <= radius_col, scores * scale, MASKED)
    weights = jnp.exp2(scores - jnp.max(scores, axis=1, keepdims=True))
    weights = weights * (1.0 / jnp.sum(weights, axis=1, keepdims=True))
    return jnp.dot(weights.astype(jnp.bfloat16), value, preferred_element_type=jnp.float32)


def near_kernel(
    table_ref,
    q_ref,
    k_ref,
    v_ref,
    outer_ref,
    inner_ref,
    before_ref,
    after_ref,
    row_far,
    frame_far,
    out_ref,
):
    columns = q_ref.shape[2]
    first, second, third = (table_ref[COUNTS + i] for i in range(3))

    def put(slot, frame, at, keys, values, far):
        result = attend(q_ref[frame, 0, :, at], keys, values, far, table_ref[COL_RADIUS + slot])
        out_ref[frame, 0, :, at] = result.astype(out_ref.dtype)

    @pl.loop(first, second)
    def _(slot):
        at = head_lanes(table_ref, slot)
        for frame in range(2):
            keys = [outer_ref[frame, slot, 0], k_ref[frame, 0, :, at], inner_ref[frame, slot, 0]]
            values = [outer_ref[frame, slot, 1], v_ref[frame, 0, :, at], inner_ref[frame, slot, 1]]
            put(slot, frame, at, keys, values, row_far[...])

    @pl.loop(second, third)
    def _(slot):
        at = head_lanes(table_ref, slot)
        for frame in range(2):
            far = frame_far[0, :, columns : 2 * columns]
            put(slot, frame, at, [k_ref[frame, 0, :, at]], [v_ref[frame, 0, :, at]], far)

    @pl.loop(third, HEADS)
    def _(slot):
        at = head_lanes(table_ref, slot)
        place = slot - third + first
        keys = [
            before_ref[place, 0],
            k_ref[0, 0, :, at],
            k_ref[1, 0, :, at],
            after_ref[place, 0],
        ]
        values = [
            before_ref[place, 1],
            v_ref[0, 0, :, at],
            v_ref[1, 0, :, at],
            after_ref[place, 1],
        ]
        for frame in range(2):
            put(
                slot,
                frame,
                at,
                keys[frame : frame + 3],
                values[frame : frame + 3],
                frame_far[frame],
            )


def far_kernel(
    table_ref,
    q_ref,
    k_ref,
    v_ref,
    outer_ref,
    inner_ref,
    before_ref,
    after_ref,
    before_outer_ref,
    after_outer_ref,
    inner_corner_ref,
    both_far,
    near_ref,
    out_ref,
):
    out_ref[...] = near_ref[...]

    @pl.loop(0, table_ref[COUNTS])
    def _(slot):
        at = head_lanes(table_ref, slot)

        def planes(kv, own_ref):
            return [
                [
                    before_outer_ref[slot, kv],
                    before_ref[slot, kv],
                    inner_corner_ref[0, slot, kv],
                ],
                [outer_ref[0, slot, kv], own_ref[0, 0, :, at], inner_ref[0, slot, kv]],
                [outer_ref[1, slot, kv], own_ref[1, 0, :, at], inner_ref[1, slot, kv]],
                [after_outer_ref[slot, kv], after_ref[slot, kv], inner_corner_ref[1, slot, kv]],
            ]

        keys, values = planes(0, k_ref), planes(1, v_ref)
        for frame in range(2):
            result = attend(
                q_ref[frame, 0, :, at],
                sum(keys[frame : frame + 3], []),
                sum(values[frame : frame + 3], []),
                both_far[frame],
                table_ref[COL_RADIUS + slot],
            )
            out_ref[frame, 0, :, at] = result.astype(out_ref.dtype)


def in_vmem(*arrays):
    return [pltpu.with_memory_space_constraint(array, pltpu.VMEM) for array in arrays]


def attention(kernel, name, table, queries, *operands):
    vmem = pl.BlockSpec(memory_space=pltpu.VMEM)
    return pl.pallas_call(
        kernel,
        in_specs=[pl.BlockSpec(memory_space=pltpu.SMEM)] + [vmem] * (1 + len(operands)),
        out_specs=vmem,
        out_shape=jax.ShapeDtypeStruct(queries.shape, queries.dtype),
        compiler_params=pltpu.CompilerParams(vmem_limit_bytes=ATTENTION_VMEM),
        cost_estimate=pl.CostEstimate(
            flops=1_500_000_000, bytes_accessed=16_000_000, transcendentals=3_000_000
        ),
        name=name,
    )(table, *in_vmem(queries, *operands))


def corners_kernel(table_ref, before_ref, after_ref, *refs):
    if len(refs) > 4:
        direct_ref, near_ref, relayed_ref, last_ref, first_ref, inner_ref, outer_ref = refs
        split = direct_ref.shape[1]
        relayed = table_ref[RELAYED] > 0
        for frame in range(2):
            outer_ref[frame, :split] = direct_ref[frame]

        @pl.when(relayed)
        def _():
            for frame in range(2):
                outer_ref[frame, split:] = relayed_ref[frame]

        @pl.when(jnp.logical_not(relayed))
        def _():
            for frame in range(2):
                outer_ref[frame, split:] = near_ref[frame]
    else:
        outer_ref, last_ref, first_ref, inner_ref = refs
    size = last_ref.shape[0]
    last_ref[...] = outer_ref[1, :size]
    first_ref[...] = outer_ref[0, :size]
    inner_ref[0] = before_ref[:size]
    inner_ref[1] = after_ref[:size]


def pack_corners(table, outer_parts, before, after, size):
    vmem = pl.BlockSpec(memory_space=pltpu.VMEM)
    edge = jax.ShapeDtypeStruct((size,) + before.shape[1:], before.dtype)
    shapes = [edge, edge, jax.ShapeDtypeStruct((2,) + edge.shape, edge.dtype)]
    if len(outer_parts) > 1:
        rows = outer_parts[0].shape[1] + outer_parts[1].shape[1]
        shape = outer_parts[0].shape
        shapes.append(jax.ShapeDtypeStruct(shape[:1] + (rows,) + shape[2:], before.dtype))
    return pl.pallas_call(
        corners_kernel,
        in_specs=[pl.BlockSpec(memory_space=pltpu.SMEM)] + [vmem] * (2 + len(outer_parts)),
        out_specs=[vmem] * len(shapes),
        out_shape=shapes,
        compiler_params=pltpu.CompilerParams(vmem_limit_bytes=20 * 1024 * 1024),
        cost_estimate=pl.CostEstimate(flops=0, bytes_accessed=6_000_000, transcendentals=0),
        name="pack_corners",
    )(table, *in_vmem(before, after, *outer_parts))


def choose_kernel(table_ref, even_ref, odd_ref, out_ref):
    odd = (table_ref[PLACE] & 1) == 1

    @pl.when(odd)
    def _():
        out_ref[...] = odd_ref[...]

    @pl.when(jnp.logical_not(odd))
    def _():
        out_ref[...] = even_ref[...]


def choose(table, even, odd):
    vmem = pl.BlockSpec(memory_space=pltpu.VMEM)
    return pl.pallas_call(
        choose_kernel,
        in_specs=[pl.BlockSpec(memory_space=pltpu.SMEM), vmem, vmem],
        out_specs=vmem,
        out_shape=jax.ShapeDtypeStruct(even.shape, even.dtype),
        compiler_params=pltpu.CompilerParams(vmem_limit_bytes=14 * 1024 * 1024),
        cost_estimate=pl.CostEstimate(flops=0, bytes_accessed=4_000_000, transcendentals=0),
        name="choose_by_kind",
    )(table, even, odd)


def shift(block, axis, step):
    count = lax.axis_size(axis)
    return lax.ppermute(block, axis, [(i, i + step) for i in range(count) if 0 <= i + step < count])


def from_outer(block):
    count = lax.axis_size("height")
    pairs = [(i, i + 1) for i in range(1, count - 1, 2)]
    return lax.ppermute(block, "height", pairs + [(j, i) for i, j in pairs])


def swap_by_kind(block, even_mask, odd_mask):
    count = lax.axis_size("height")
    pairs = [(i, i ^ (odd_mask if i & 1 else even_mask)) for i in range(count)]
    return lax.ppermute(block, "height", pairs)


def swap(block, axis, mask):
    return lax.ppermute(block, axis, [(i, i ^ mask) for i in range(lax.axis_size(axis))])


ACROSS = (((1,), (1,)), ((), ()))


def by_kind(table_ref, body):
    odd = (table_ref[PLACE] & 1) == 1
    pl.when(jnp.logical_not(odd))(lambda: body(0))
    pl.when(odd)(lambda: body(1))


def chip_columns(table_ref, mask, width):
    return pl.ds(pl.multiple_of(((table_ref[PLACE] >> 1) ^ mask) * width, width), width)


def project_kernel(masks, table_ref, attended_ref, cotangent_ref, *refs):
    chips, closing = len(masks), len(masks) == 1
    pieces, refs = refs[: 2 * chips], refs[2 * chips :]
    low_ref, up_ref, back_low_ref, down_ref = refs[:4]
    partial_ref = refs[4]
    mixed_ref, gradient_ref, rows, total = refs[-4:]
    width, step = 2 * pieces[0].shape[0], 512

    for c in range(chips):
        at = chip_columns(table_ref, masks[c], width)
        rows[:, c * width : (c + 1) * width] = attended_ref[:, at]
        total[:, c * width : (c + 1) * width] = ADAPTER_SCALE * jnp.dot(
            back_low_ref[...], down_ref[:, at], preferred_element_type=jnp.float32
        )

    def body(kind):
        ordered = [pieces[2 * c + (i ^ kind)] for c in range(chips) for i in range(2)]

        @pl.loop(0, mixed_ref.shape[1] // step)
        def _(n):
            at = pl.ds(pl.multiple_of(n * step, step), step)
            weight = jnp.concatenate([piece[:, at] for piece in ordered], axis=0)
            mixed = jnp.dot(rows[...], weight, preferred_element_type=jnp.float32)
            if closing:
                mixed += partial_ref[:, at]
            else:
                mixed += ADAPTER_SCALE * jnp.dot(
                    low_ref[...], up_ref[:, at], preferred_element_type=jnp.float32
                )
            mixed_ref[:, at] = mixed.astype(mixed_ref.dtype)
            total[...] += lax.dot_general(
                cotangent_ref[:, at], weight, ACROSS, preferred_element_type=jnp.float32
            )

    by_kind(table_ref, body)

    if closing:
        gradient_ref[...] = total[...].astype(gradient_ref.dtype)
    else:
        for c in range(chips):
            part = total[:, c * width : (c + 1) * width]
            at = chip_columns(table_ref, masks[c], width)
            gradient_ref[:, at] = part.astype(gradient_ref.dtype)


def project(table, attended, cotangent, pieces, adapters, masks, partial=None):
    tokens, features = attended.shape
    width = 2 * pieces[0].shape[0]
    closing = partial is not None
    assert closing == (len(masks) == 1)
    vmem = pl.BlockSpec(memory_space=pltpu.VMEM)
    operands = in_vmem(attended, cotangent, *pieces, *adapters)
    specs = [vmem] * len(operands)
    if closing:
        operands += in_vmem(partial[0]) + [partial[1]]
        specs += [vmem, pl.BlockSpec(memory_space=pl.ANY)]
        gradient_block = pl.BlockSpec(
            (tokens, width), lambda n, t: (0, (t[PLACE] >> 1) ^ masks[0])
        )
        mixed_type = cotangent.dtype
    else:
        gradient_block = vmem
        mixed_type = jnp.float32
    return pl.pallas_call(
        functools.partial(project_kernel, masks),
        grid_spec=pltpu.PrefetchScalarGridSpec(
            num_scalar_prefetch=1,
            grid=(1,),
            in_specs=specs,
            out_specs=[vmem, gradient_block],
            scratch_shapes=[
                pltpu.VMEM((tokens, len(masks) * width), attended.dtype),
                pltpu.VMEM((tokens, len(masks) * width), jnp.float32),
            ],
        ),
        out_shape=[
            jax.ShapeDtypeStruct(cotangent.shape, mixed_type),
            jax.ShapeDtypeStruct(attended.shape, attended.dtype),
        ],
        input_output_aliases={8 + len(pieces): 1} if closing else {},
        compiler_params=pltpu.CompilerParams(vmem_limit_bytes=24 * 1024 * 1024),
        cost_estimate=pl.CostEstimate(
            flops=2_200_000_000 * len(masks),
            bytes_accessed=5_000_000 * len(masks),
            transcendentals=0,
        ),
        name="project_last" if closing else "project_first",
    )(table, *operands)


def sum_everywhere(total, sides, before_frames, before_spread, before_twin):
    rows_count, frames_count = lax.axis_size("height"), lax.axis_size("tm")
    masks = [1 << b for b in range(rows_count.bit_length() - 1)]
    is_upper = lambda mask: sides[mask.bit_length() - 1] > 0
    for mask in masks:
        half = total.shape[0] // 2
        upper = is_upper(mask)
        send = jnp.where(upper, total[:half], total[half:])
        keep = jnp.where(upper, total[half:], total[:half])
        if mask == 1:
            total = keep + swap(send, "height", mask)
        else:
            total = keep + swap(send.astype(jnp.bfloat16), "height", mask).astype(jnp.float32)
    total = before_frames(total)
    for b in range(frames_count.bit_length() - 1):
        total = total.astype(jnp.bfloat16)
        total = total.astype(jnp.float32) + swap(total, "tm", 1 << b).astype(jnp.float32)
    total = before_spread(total.astype(jnp.bfloat16))
    for mask in reversed(masks):
        upper = is_upper(mask)
        if mask == 1:
            total = before_twin(total)
        other = swap(total, "height", mask)
        total = jnp.concatenate(
            [jnp.where(upper, other, total), jnp.where(upper, total, other)], axis=0
        )
    return total.astype(jnp.float32)


def branch(row_size, frame_size, corner_size):
    def run(
        table,
        queries,
        keys,
        values,
        output_weight,
        adapter_down_weight,
        adapter_up_weight,
        output_gradient,
    ):
        frames, row_total, column_count, feature_width = queries.shape
        out_width = output_gradient.shape[3]
        token_count = frames * row_total * column_count
        ring = lax.axis_size("height") == 8
        rows, last, first = pack(table, keys, values, row_size, frame_size, ring)
        if ring:
            rows, direct, rest = rows
            hop = lax.ppermute(
                rest, "height", [(1, 2), (2, 1), (5, 6), (6, 5), (3, 7), (4, 0)]
            )
            outer_parts = (
                from_outer(direct),
                hop,
                lax.ppermute(hop, "height", [(7, 4), (0, 3)]),
            )
        else:
            rows = rows[0]
            outer_parts = (from_outer(rows),)
        inner = swap(rows, "height", 1)
        before = shift(last, "tm", 1)
        after = shift(first, "tm", -1)
        output_cotangent = output_gradient.reshape(token_count, out_width)
        low_rank_backward = lax.dot_general(
            output_cotangent,
            adapter_up_weight,
            ACROSS,
            preferred_element_type=jnp.float32,
        ).astype(jnp.bfloat16)
        masks = make_masks(
            table, column_count, lax.axis_size("height").bit_length() - 1, out_width
        )
        outer_parts, inner, before, after, shard, low_rank_backward, masks = (
            lax.optimization_barrier(
                (outer_parts, inner, before, after, output_weight, low_rank_backward, masks)
            )
        )
        row_far, frame_far, both_far, sides = masks
        outer_last, outer_first, own_edges, *joined = pack_corners(
            table, outer_parts, before, after, corner_size
        )
        outer = joined[0] if joined else outer_parts[0]
        before_outer = shift(outer_last, "tm", 1)
        after_outer = shift(outer_first, "tm", -1)
        inner_corners = swap(own_edges, "height", 1)
        near = attention(
            near_kernel,
            "attention_near",
            table,
            queries,
            keys,
            values,
            outer,
            inner,
            before,
            after,
            row_far,
            frame_far,
        )
        corners = (before_outer, after_outer, inner_corners)
        if ring:
            over_x = swap(shard, "height", 2)
            over_y = swap(shard, "height", 4)
        else:
            weight = lax.all_gather(shard, "height", axis=0, tiled=True)
        corners, near = lax.optimization_barrier((corners, near))
        attended = attention(
            far_kernel,
            "attention_far",
            table,
            queries,
            keys,
            values,
            outer,
            inner,
            before,
            after,
            *corners,
            both_far,
            near,
        )
        if ring:
            attended, over_x, over_y, shard = lax.optimization_barrier(
                (attended, over_x, over_y, shard)
            )
            twin = swap(shard, "height", 1)
            twin_x = swap(over_x, "height", 1)
            twin_y = swap(over_y, "height", 1)
            over_both = choose(table, over_y, over_x)
        attention_output = attended.reshape(token_count, feature_width)
        low_rank_product = jnp.dot(
            attention_output, adapter_down_weight, preferred_element_type=jnp.float32
        ).astype(jnp.bfloat16)
        token_total = token_count * lax.axis_size("tm") * lax.axis_size("height")
        adapter_factor = ADAPTER_SCALE / math.sqrt(token_total)
        local_up = lax.dot_general(
            low_rank_product,
            output_cotangent,
            (((0,), (0,)), ((), ())),
            preferred_element_type=jnp.float32,
        )
        local_down = lax.dot_general(
            low_rank_backward,
            attention_output,
            (((0,), (0,)), ((), ())),
            preferred_element_type=jnp.float32,
        )
        held = {}

        adapters = (
            low_rank_product,
            adapter_up_weight,
            low_rank_backward,
            adapter_down_weight.T,
        )

        def send_last(total):
            if ring:
                total, last_shard = lax.optimization_barrier((total, over_both))
                held["last"] = swap_by_kind(last_shard, 2, 4)
            return total

        def arrived(total):
            if ring:
                partial = project(
                    table,
                    attention_output,
                    output_cotangent,
                    (output_weight, twin, over_x, twin_x, over_y, twin_y),
                    adapters,
                    (0, 1, 2),
                )
                total, held["last"], held["partial"] = lax.optimization_barrier(
                    (total, held["last"], partial)
                )
                held["last_twin"] = swap(held["last"], "height", 1)
            return total

        def complete(total):
            if ring:
                total, held["last_twin"] = lax.optimization_barrier((total, held["last_twin"]))
            return total

        grads = adapter_factor * sum_everywhere(
            jnp.concatenate([local_up, local_down], axis=0), sides, send_last, arrived, complete
        )
        rank = local_up.shape[0]
        grad_up, grad_down = grads[:rank], grads[rank:].T
        if ring:
            mixed, attention_gradient = project(
                table,
                attention_output,
                output_cotangent,
                (held["last"], held["last_twin"]),
                adapters,
                (3,),
                held["partial"],
            )
        else:
            mixed = jnp.dot(
                attention_output, weight, preferred_element_type=jnp.float32
            ) + ADAPTER_SCALE * jnp.dot(
                low_rank_product, adapter_up_weight, preferred_element_type=jnp.float32
            )
            attention_gradient = lax.dot_general(
                output_cotangent, weight, ACROSS, preferred_element_type=jnp.float32
            ) + ADAPTER_SCALE * lax.dot_general(
                low_rank_backward, adapter_down_weight, ACROSS, preferred_element_type=jnp.float32
            )
        mixed = mixed.astype(jnp.bfloat16).reshape(frames, row_total, column_count, out_width)
        attention_gradient = attention_gradient.astype(jnp.bfloat16).reshape(
            frames, row_total, column_count, feature_width
        )
        return (mixed, attention_gradient, grad_up, grad_down)

    return run


def per_device(
    queries,
    keys,
    values,
    head_window_radius,
    output_weight,
    adapter_down_weight,
    adapter_up_weight,
    output_gradient,
):
    table = head_table(head_window_radius)
    tier = table[TIER]
    return lax.switch(
        tier,
        [branch(*sizes) for sizes in TIERS],
        table,
        queries,
        keys,
        values,
        output_weight,
        adapter_down_weight,
        adapter_up_weight,
        output_gradient,
    )


def solution(mesh):
    in_specs = (
        P("tm", "height", None, None),
        P("tm", "height", None, None),
        P("tm", "height", None, None),
        P(),
        P("height", None),
        P(),
        P(),
        P("tm", "height", None, None),
    )
    out_specs = (P("tm", "height", None, None), P("tm", "height", None, None), P(), P())
    return jax.shard_map(
        per_device, mesh=mesh, in_specs=in_specs, out_specs=out_specs, check_vma=False
    )
```

time: 589 us -> 144 us (0.24)
  waiting for transfers between devices: 340 us -> 57.1 us
  matrix products: 140 us -> 2.04 us
  Pallas kernels: 0 us -> 48 us
  local copies, waits for them, and re-layouts: 40.2 us -> 2.28 us
  other arithmetic: 38.3 us -> 1.27 us
  starting transfers between devices: 11.8 us -> 31.1 us
  between operations: 15.7 us -> 1.33 us
    psum x1 -> x0, waiting for transfers between devices: 293 us -> none  [per_device(): grad_up, grad_down = lax.psum((local_up, local_down), ('tm', 'height'))]
    dot_general x48 -> x4, matrix products: 140 us -> 2.04 us  [the longest x1 0.56 us: run(): jnp.dot(attention_output, adapter_down_weight, preferred_element_type=jnp...]
    pallas_call x0 -> x10, Pallas kernels: none -> 48 us  [the longest x2 23.9 us: attention(): pl.pallas_call(kernel, in_specs=[pl.BlockSpec(memory_space=pltpu.SMEM)] +...]
    slice x23 -> x1, local copies, waits for them, and re-layouts: 33.6 us -> 0.58 us  [per_device(): tier = table[TIER]]
    ppermute x4 -> x24, starting transfers between devices: 11.8 us -> 31.1 us  [the longest x16 15 us: swap(): lax.ppermute(block, axis, [(i, i ^ mask) for i in range(lax.axis_size(axi...]
    le x20 -> x0, other arithmetic: 13 us -> none  [one_head(): diff_row <= radius[1]]
    concatenate x2, other arithmetic: 13 us -> 0.04 us  [sum_everywhere(): jnp.concatenate([jnp.where(upper, other, total), jnp.where(upper, total,...]
    ppermute x4 -> x24, waiting for transfers between devices: 46.5 us -> 57.1 us  [the longest x16 29.5 us: swap(): lax.ppermute(block, axis, [(i, i ^ mask) for i in range(lax.axis_size(axi...]
  transfers between devices with their start and end apart: 6 -> 24, of which waited for: 5 -> 15; matrix products, arithmetic and copies ran while one was open for 36% -> 1% of each run, Pallas kernels for 0% -> 30%
where the time goes in v1:
time: 144 us
  waiting for transfers between devices  57.1 us (40%)
  Pallas kernels  48 us (33%)
  starting transfers between devices  31.1 us (22%)
  local copies, waits for them, and re-layouts  2.28 us (2%)
  matrix products  2.04 us (1%)
    ppermute x16, waiting for transfers between devices, swap(): lax.ppermute(block, axis, [(i, i ^ mask) for i in range(lax.axis_size(axi...  29.5 us
    pallas_call x2, Pallas kernels, attention(): pl.pallas_call(kernel, in_specs=[pl.BlockSpec(memory_space=pltpu.SMEM)] +...  23.9 us
    ppermute x4, waiting for transfers between devices, shift(): lax.ppermute(block, axis, [(i, i + step) for i in range(count) if 0 <= i...  17.7 us
    pallas_call x2, Pallas kernels, project(): pl.pallas_call(functools.partial(project_kernel, masks), grid_spec=pltpu....  15.3 us
    ppermute x16, starting transfers between devices, swap(): lax.ppermute(block, axis, [(i, i ^ mask) for i in range(lax.axis_size(axi...  15 us
    ppermute x4, starting transfers between devices, shift(): lax.ppermute(block, axis, [(i, i + step) for i in range(count) if 0 <= i...  10.8 us
    ppermute x1, waiting for transfers between devices, run(): lax.ppermute(rest, 'height', [(1, 2), (2, 1), (5, 6), (6, 5), (3, 7), (4,...  6.72 us
  transfers between devices with their start and end apart: 24, of which 15 were waited for; matrix products, arithmetic and copies ran while one was open for 1% of the time, Pallas kernels for 30%

profile of v1, /device:TPU:0, one launch (start us, length us, event | category | flops | bytes accessed | tf_op | source)
XLA Modules:
  0.0 143.8 jit_solution(15353690013952248381)
XLA Ops:
  1.2 2.5 %head_table.1 = s32[49]{0:T(128)S(1)} custom-call(s32[4]{0:T(128)} %pad_add_fusion.places_ref, s32[3,20]{1,0:T(4,128)} %bitcast.60), custom_call_target="tpu_custom_call" | custom-call | tf_op jit(solution)/shard_map/head_table/pallas_call | solution.py:78
  5.0 137.2 %conditional.1 = (bf16[2,1,160,2560]{3,2,0,1:T(8,128)(2,1)S(1)}, bf16[2,1,160,2560]{3,2,0,1:T(8,128)(2,1)}, f32[64,2560]{1,0:T(8,128)S(1)}, f32[2560,64]{0,1:T(8,128)S(1)}) conditional(s32[]{:T(128)} %bitcast.19, (s32[49]{0:T(128)S(1)}, bf16[2,1,160,2560]{3,2,1,0:T(8,128)(2,1)}, bf16[2,1,160,2560]{3,2,1,0:T(8,128)(2,1)}, ...), branch_computations={%region_0.1_spmd, %region_1.2_spmd} | conditional | flops 12224333824 | bytes 267317568 | solution.py:766
  5.2 2.7 %pack_rows.3 = (bf16[2,13,2,160,128]{4,3,2,1,0:T(8,128)(2,1)S(1)}, bf16[2,7,2,160,128]{4,3,2,1,0:T(8,128)(2,1)S(1)}, bf16[2,6,2,160,128]{4,3,2,1,0:T(8,128)(2,1)S(1)}) custom-call(s32[49]{0:T(128)S(1)} %get-tuple-element.85.table_ref, bf16[2,1,160,2560]{3,2,1,0:T(8,128)(2,1)} %get-tuple-element.87.keys_ref.k_ref, ...), custom_call_target="tpu_custom_call" | custom-call | bytes 8000000 | tf_op jit(solution)/shard_map/cond/branch_1_fun/pack_rows/pallas_call | solution.py:132
  8.5 1.4 collective-permute-start.25
  9.9 1.2 pack_edges.3
  11.1 4.7 %collective-permute-start.28 = (bf16[14,2,160,128]{3,2,1,0:T(8,128)(2,1)S(1)}, bf16[14,2,160,128]{3,2,1,0:T(8,128)(2,1)S(1)}, u32[]{:S(2)}, u32[]{:S(2)}) collective-permute-start(bf16[14,2,160,128]{3,2,1,0:T(8,128)(2,1)S(1)} %get-tuple-element.92), channel_id=1, source_target_pairs={{0,8},{8,16},{16,24},{1,9},{9,17},{17,25},{2,10},{10,18},{18,26},{... | collective-permute-start | bytes 3440648 | tf_op jit(solution)/shard_map/cond/branch_1_fun/ppermute | solution.py:415
  15.8 1.3 collective-permute-start.29
  17.9 6.7 %collective-permute-done.25.refs_1_ = bf16[2,6,2,160,128]{4,3,2,1,0:T(8,128)(2,1)S(1)} collective-permute-done((bf16[2,6,2,160,128]{4,3,2,1,0:T(8,128)(2,1)S(1)}, bf16[2,6,2,160,128]{4,3,2,1,0:T(8,128)(2,1)S(1)}, u32[]{:S(2)}, u32[]{:S(2)}) %collective-permute-start.25) | collective-permute-done | bytes 983072 | tf_op jit(solution)/shard_map/cond/branch_1_fun/ppermute | solution.py:584
  24.6 2.7 %collective-permute-start.26 = (bf16[2,6,2,160,128]{4,3,2,1,0:T(8,128)(2,1)S(1)}, bf16[2,6,2,160,128]{4,3,2,1,0:T(8,128)(2,1)S(1)}, u32[]{:S(2)}, u32[]{:S(2)}) collective-permute-start(bf16[2,6,2,160,128]{4,3,2,1,0:T(8,128)(2,1)S(1)} %collective-permute-done.25.refs_1_), channel_id=1, source_target_pairs={{7,4},{0,3},{15,12},{8,11},{23,20},{16,19},{31,28},{24,27}} | collective-permute-start | bytes 2949128 | tf_op jit(solution)/shard_map/cond/branch_1_fun/ppermute | solution.py:590
  28.7 11.4 %collective-permute-done.28.before_ref = bf16[14,2,160,128]{3,2,1,0:T(8,128)(2,1)S(1)} collective-permute-done((bf16[14,2,160,128]{3,2,1,0:T(8,128)(2,1)S(1)}, bf16[14,2,160,128]{3,2,1,0:T(8,128)(2,1)S(1)}, u32[]{:S(2)}, u32[]{:S(2)}) %collective-permute-start.28) | collective-permute-done | bytes 1146912 | tf_op jit(solution)/shard_map/cond/branch_1_fun/ppermute | solution.py:415
  40.1 4.8 %collective-permute-done.29.after_ref = bf16[14,2,160,128]{3,2,1,0:T(8,128)(2,1)S(1)} collective-permute-done((bf16[14,2,160,128]{3,2,1,0:T(8,128)(2,1)S(1)}, bf16[14,2,160,128]{3,2,1,0:T(8,128)(2,1)S(1)}, u32[]{:S(2)}, u32[]{:S(2)}) %collective-permute-start.29) | collective-permute-done | bytes 1146912 | tf_op jit(solution)/shard_map/cond/branch_1_fun/ppermute | solution.py:415
  44.9 2.0 %collective-permute-done.26.refs_2_ = bf16[2,6,2,160,128]{4,3,2,1,0:T(8,128)(2,1)S(1)} collective-permute-done((bf16[2,6,2,160,128]{4,3,2,1,0:T(8,128)(2,1)S(1)}, bf16[2,6,2,160,128]{4,3,2,1,0:T(8,128)(2,1)S(1)}, u32[]{:S(2)}, u32[]{:S(2)}) %collective-permute-start.26) | collective-permute-done | bytes 983072 | tf_op jit(solution)/shard_map/cond/branch_1_fun/ppermute | solution.py:590
  46.9 2.4 %collective-permute-start.33 = (bf16[320,2560]{1,0:T(8,128)(2,1)S(1)}, bf16[320,2560]{1,0:T(8,128)(2,1)S(1)}, u32[]{:S(2)}, u32[]{:S(2)}) collective-permute-start(bf16[320,2560]{1,0:T(8,128)(2,1)S(1)} %copy-done.13), channel_id=1, source_target_pairs={{0,2},{1,3},{2,0},{3,1},{4,6},{5,7},{6,4},{7,5},{8,10},{9,11},{10,... | collective-permute-start | bytes 4915208 | tf_op jit(solution)/shard_map/cond/branch_1_fun/ppermute | solution.py:431
  49.3 3.4 %collective-permute-start.34 = (bf16[320,2560]{1,0:T(8,128)(2,1)S(1)}, bf16[320,2560]{1,0:T(8,128)(2,1)S(1)}, u32[]{:S(2)}, u32[]{:S(2)}) collective-permute-start(bf16[320,2560]{1,0:T(8,128)(2,1)S(1)} %copy-done.13), channel_id=1, source_target_pairs={{0,4},{1,5},{2,6},{3,7},{4,0},{5,1},{6,2},{7,3},{8,12},{9,13},{10,... | collective-permute-start | bytes 4915208 | tf_op jit(solution)/shard_map/cond/branch_1_fun/ppermute | solution.py:431
  53.7 3.5 %collective-permute-start.30 = (bf16[9,2,160,128]{3,2,1,0:T(8,128)(2,1)S(1)}, bf16[9,2,160,128]{3,2,1,0:T(8,128)(2,1)S(1)}, u32[]{:S(2)}, u32[]{:S(2)}) collective-permute-start(bf16[9,2,160,128]{3,2,1,0:T(8,128)(2,1)S(1)} %get-tuple-element.108), channel_id=1, source_target_pairs={{0,8},{8,16},{16,24},{1,9},{9,17},{17,25},{2,10},{10,18},{18,26},{... | collective-permute-start | bytes 2211848 | tf_op jit(solution)/shard_map/cond/branch_1_fun/ppermute | solution.py:415
  57.2 1.3 collective-permute-start.31
  58.6 17.5 %attention_near.3.near_ref = bf16[2,1,160,2560]{3,2,1,0:T(8,128)(2,1)S(1)} custom-call(s32[49]{0:T(128)S(1)} %get-tuple-element.85.table_ref, bf16[2,1,160,2560]{3,2,1,0:T(8,128)(2,1)S(1)} %copy-done.5, bf16[2,1,160,2560]{3,2,1,0:T(8,128)(2,1)S(1)} %copy-done.1, bf16[2,1,160,2560]{3,2,1,0:T(8,128)(2,1)S(1)} %copy-done.3, ...), custom_call_target="tpu_custom_call" | custom-call | flops 1500000000 | bytes 16000000 | tf_op jit(solution)/shard_map/cond/branch_1_fun/attention_near/pallas_call | solution.py:330
  76.2 1.5 %collective-permute-done.31.after_outer_ref = bf16[9,2,160,128]{3,2,1,0:T(8,128)(2,1)S(1)} collective-permute-done((bf16[9,2,160,128]{3,2,1,0:T(8,128)(2,1)S(1)}, bf16[9,2,160,128]{3,2,1,0:T(8,128)(2,1)S(1)}, u32[]{:S(2)}, u32[]{:S(2)}) %collective-permute-start.31) | collective-permute-done | bytes 737312 | tf_op jit(solution)/shard_map/cond/branch_1_fun/ppermute | solution.py:415
  77.7 6.4 %attention_far.3 = bf16[2,1,160,2560]{3,2,1,0:T(8,128)(2,1)S(1)} custom-call(s32[49]{0:T(128)S(1)} %get-tuple-element.85.table_ref, bf16[2,1,160,2560]{3,2,1,0:T(8,128)(2,1)S(1)} %copy-done.5, bf16[2,1,160,2560]{3,2,1,0:T(8,128)(2,1)S(1)} %copy-done.1, bf16[2,1,160,2560]{3,2,1,0:T(8,128)(2,1)S(1)} %copy-done.3, ...), custom_call_target="tpu_custom_call" | custom-call | flops 1500000000 | bytes 16000000 | tf_op jit(solution)/shard_map/cond/branch_1_fun/attention_far/pallas_call | solution.py:330
  84.6 4.1 %collective-permute-done.34.even_ref.refs_4_ = bf16[320,2560]{1,0:T(8,128)(2,1)S(1)} collective-permute-done((bf16[320,2560]{1,0:T(8,128)(2,1)S(1)}, bf16[320,2560]{1,0:T(8,128)(2,1)S(1)}, u32[]{:S(2)}, u32[]{:S(2)}) %collective-permute-start.34) | collective-permute-done | bytes 1638432 | tf_op jit(solution)/shard_map/cond/branch_1_fun/ppermute | solution.py:431
  90.2 2.1 %collective-permute-done.35 = f32[64,2560]{1,0:T(8,128)S(1)} collective-permute-done((f32[64,2560]{1,0:T(8,128)S(1)}, f32[64,2560]{1,0:T(8,128)S(1)}, u32[]{:S(2)}, u32[]{:S(2)}) %collective-permute-start.35) | collective-permute-done | bytes 655392 | tf_op jit(solution)/shard_map/cond/branch_1_fun/ppermute | solution.py:431
  92.9 5.8 %collective-permute-done.36 = bf16[32,2560]{1,0:T(8,128)(2,1)S(1)} collective-permute-done((bf16[32,2560]{1,0:T(8,128)(2,1)S(1)}, bf16[32,2560]{1,0:T(8,128)(2,1)S(1)}, u32[]{:S(2)}, u32[]{:S(2)}) %collective-permute-start.36) | collective-permute-done | bytes 163872 | tf_op jit(solution)/shard_map/cond/branch_1_fun/ppermute | solution.py:431
  100.4 2.9 %collective-permute-done.37 = bf16[16,2560]{1,0:T(8,128)(2,1)S(1)} collective-permute-done((bf16[16,2560]{1,0:T(8,128)(2,1)S(1)}, bf16[16,2560]{1,0:T(8,128)(2,1)S(1)}, u32[]{:S(2)}, u32[]{:S(2)}) %collective-permute-start.37) | collective-permute-done | bytes 81952 | tf_op jit(solution)/shard_map/cond/branch_1_fun/ppermute | solution.py:431
  103.4 2.3 %collective-permute-start.38 = (bf16[16,2560]{1,0:T(8,128)(2,1)S(1)}, bf16[16,2560]{1,0:T(8,128)(2,1)S(1)}, u32[]{:S(2)}, u32[]{:S(2)}) collective-permute-start(bf16[16,2560]{1,0:T(8,128)(2,1)S(1)} %convert_add_fusion.3), channel_id=1, source_target_pairs={{0,8},{8,0},{16,24},{24,16},{1,9},{9,1},{17,25},{25,17},{2,10},{10... | collective-permute-start | bytes 245768 | tf_op jit(solution)/shard_map/cond/branch_1_fun/ppermute | solution.py:431
  106.1 1.9 %collective-permute-done.38 = bf16[16,2560]{1,0:T(8,128)(2,1)S(1)} collective-permute-done((bf16[16,2560]{1,0:T(8,128)(2,1)S(1)}, bf16[16,2560]{1,0:T(8,128)(2,1)S(1)}, u32[]{:S(2)}, u32[]{:S(2)}) %collective-permute-start.38) | collective-permute-done | bytes 81952 | tf_op jit(solution)/shard_map/cond/branch_1_fun/ppermute | solution.py:431
  108.1 3.8 %collective-permute-start.39 = (bf16[16,2560]{1,0:T(8,128)(2,1)S(1)}, bf16[16,2560]{1,0:T(8,128)(2,1)S(1)}, u32[]{:S(2)}, u32[]{:S(2)}) collective-permute-start(bf16[16,2560]{1,0:T(8,128)(2,1)S(1)} %add_convert_fusion.3), channel_id=1, source_target_pairs={{0,16},{8,24},{16,0},{24,8},{1,17},{9,25},{17,1},{25,9},{2,18},{10... | collective-permute-start | bytes 245768 | tf_op jit(solution)/shard_map/cond/branch_1_fun/ppermute | solution.py:431
  111.9 3.3 %collective-permute-done.39 = bf16[16,2560]{1,0:T(8,128)(2,1)S(1)} collective-permute-done((bf16[16,2560]{1,0:T(8,128)(2,1)S(1)}, bf16[16,2560]{1,0:T(8,128)(2,1)S(1)}, u32[]{:S(2)}, u32[]{:S(2)}) %collective-permute-start.39) | collective-permute-done | bytes 81952 | tf_op jit(solution)/shard_map/cond/branch_1_fun/ppermute | solution.py:431
  115.3 10.3 %project_first.3 = (f32[320,2560]{1,0:T(8,128)S(1)}, bf16[320,2560]{1,0:T(8,128)(2,1)}) custom-call(s32[49]{0:T(128)S(1)} %get-tuple-element.85.table_ref, bf16[320,2560]{1,0:T(8,128)(2,1)S(1)} %bitcast.54, bf16[320,2560]{1,0:T(8,128)(2,1)S(1)} %bitcast.46, bf16[320,2560]{1,0:T(8,128)(2,1)S(1)} %copy-done.13, ...), custom_call_target="tpu_custom_call" | custom-call | flops 6600000000 | bytes 15000000 | tf_op jit(solution)/shard_map/cond/branch_1_fun/project_first/pallas_call | solution.py:510
  125.5 1.3 collective-permute-done.40.refs_0_
  127.2 4.0 %collective-permute-done.44 = bf16[16,2560]{1,0:T(8,128)(2,1)S(1)} collective-permute-done((bf16[16,2560]{1,0:T(8,128)(2,1)S(1)}, bf16[16,2560]{1,0:T(8,128)(2,1)S(1)}, u32[]{:S(2)}, u32[]{:S(2)}) %collective-permute-start.44) | collective-permute-done | bytes 81952 | tf_op jit(solution)/shard_map/cond/branch_1_fun/ppermute | solution.py:431
  131.8 4.8 %collective-permute-done.45 = bf16[32,2560]{1,0:T(8,128)(2,1)S(1)} collective-permute-done((bf16[32,2560]{1,0:T(8,128)(2,1)S(1)}, bf16[32,2560]{1,0:T(8,128)(2,1)S(1)}, u32[]{:S(2)}, u32[]{:S(2)}) %collective-permute-start.45) | collective-permute-done | bytes 163872 | tf_op jit(solution)/shard_map/cond/branch_1_fun/ppermute | solution.py:431
  136.8 5.0 %project_last.3 = (bf16[320,2560]{1,0:T(8,128)(2,1)S(1)}, bf16[320,2560]{1,0:T(8,128)(2,1)}) custom-call(s32[49]{0:T(128)S(1)} %get-tuple-element.85.table_ref, bf16[320,2560]{1,0:T(8,128)(2,1)S(1)} %bitcast.55, bf16[320,2560]{1,0:T(8,128)(2,1)S(1)} %bitcast.47, ...), custom_call_target="tpu_custom_call", output_to_operand_aliasing={{1}: (10, {})} | custom-call | flops 2200000000 | bytes 5000000 | tf_op jit(solution)/shard_map/cond/branch_1_fun/project_last/pallas_call | solution.py:510
  (68 shorter events, 12.7 us)
Async XLA Ops:
  5.2 4.7 %copy-start.1 = (bf16[2,1,160,2560]{3,2,1,0:T(8,128)(2,1)S(1)}, bf16[2,1,160,2560]{3,2,1,0:T(8,128)(2,1)}, u32[]{:S(2)}) copy-start(bf16[2,1,160,2560]{3,2,1,0:T(8,128)(2,1)} %get-tuple-element.87.keys_ref.k_ref) | copy-start | bytes 4915204 | tf_op jit(solution)/shard_map/cond
  5.2 4.7 %copy-start.3 = (bf16[2,1,160,2560]{3,2,1,0:T(8,128)(2,1)S(1)}, bf16[2,1,160,2560]{3,2,1,0:T(8,128)(2,1)}, u32[]{:S(2)}) copy-start(bf16[2,1,160,2560]{3,2,1,0:T(8,128)(2,1)} %get-tuple-element.88.values_ref.v_ref) | copy-start | bytes 4915204 | tf_op jit(solution)/shard_map/cond
  8.0 38.9 %collective-permute-start.27 = (bf16[2,13,2,160,128]{4,3,2,1,0:T(8,128)(2,1)S(1)}, bf16[2,13,2,160,128]{4,3,2,1,0:T(8,128)(2,1)S(1)}, u32[]{:S(2)}, u32[]{:S(2)}) collective-permute-start(bf16[2,13,2,160,128]{4,3,2,1,0:T(8,128)(2,1)S(1)} %get-tuple-element.91.rows_ref), channel_id=1, source_target_pairs={{0,1},{1,0},{2,3},{3,2},{4,5},{5,4},{6,7},{7,6},{8,9},{9,8},{10,11... | collective-permute-start | bytes 6389768 | tf_op jit(solution)/shard_map/cond/branch_1_fun/ppermute | solution.py:431
  8.5 19.7 %copy-start.7 = (bf16[2,1,160,2560]{3,2,1,0:T(8,128)(2,1)S(1)}, bf16[2,1,160,2560]{3,2,1,0:T(8,128)(2,1)}, u32[]{:S(2)}) copy-start(bf16[2,1,160,2560]{3,2,1,0:T(8,128)(2,1)} %get-tuple-element.157) | copy-start | bytes 4915204 | tf_op jit(solution)/shard_map/cond
  8.5 19.7 %copy-start.9 = (bf16[64,2560]{1,0:T(8,128)(2,1)S(1)}, bf16[64,2560]{1,0:T(8,128)(2,1)}, u32[]{:S(2)}) copy-start(bf16[64,2560]{1,0:T(8,128)(2,1)} %get-tuple-element.96.refs_7_.refs_3_) | copy-start | bytes 983044 | tf_op jit(solution)/shard_map/cond
  8.5 16.1 %collective-permute-start.25 = (bf16[2,6,2,160,128]{4,3,2,1,0:T(8,128)(2,1)S(1)}, bf16[2,6,2,160,128]{4,3,2,1,0:T(8,128)(2,1)S(1)}, u32[]{:S(2)}, u32[]{:S(2)}) collective-permute-start(bf16[2,6,2,160,128]{4,3,2,1,0:T(8,128)(2,1)S(1)} %get-tuple-element.90), channel_id=1, source_target_pairs={{1,2},{2,1},{5,6},{6,5},{3,7},{4,0},{9,10},{10,9},{13,14},{14,13},... | collective-permute-start | bytes 2949128 | tf_op jit(solution)/shard_map/cond/branch_1_fun/ppermute | solution.py:584
  11.1 35.8 %copy-start.13 = (bf16[320,2560]{1,0:T(8,128)(2,1)S(1)}, bf16[320,2560]{1,0:T(8,128)(2,1)}, u32[]{:S(2)}) copy-start(bf16[320,2560]{1,0:T(8,128)(2,1)} %get-tuple-element.127.refs_0_) | copy-start | bytes 4915204 | tf_op jit(solution)/shard_map/cond
  11.1 29.0 %collective-permute-start.28 = (bf16[14,2,160,128]{3,2,1,0:T(8,128)(2,1)S(1)}, bf16[14,2,160,128]{3,2,1,0:T(8,128)(2,1)S(1)}, u32[]{:S(2)}, u32[]{:S(2)}) collective-permute-start(bf16[14,2,160,128]{3,2,1,0:T(8,128)(2,1)S(1)} %get-tuple-element.92), channel_id=1, source_target_pairs={{0,8},{8,16},{16,24},{1,9},{9,17},{17,25},{2,10},{10,18},{18,26},{... | collective-permute-start | bytes 3440648 | tf_op jit(solution)/shard_map/cond/branch_1_fun/ppermute | solution.py:415
  15.8 29.1 %collective-permute-start.29 = (bf16[14,2,160,128]{3,2,1,0:T(8,128)(2,1)S(1)}, bf16[14,2,160,128]{3,2,1,0:T(8,128)(2,1)S(1)}, u32[]{:S(2)}, u32[]{:S(2)}) collective-permute-start(bf16[14,2,160,128]{3,2,1,0:T(8,128)(2,1)S(1)} %get-tuple-element.93), channel_id=1, source_target_pairs={{8,0},{16,8},{24,16},{9,1},{17,9},{25,17},{10,2},{18,10},{26,18},{... | collective-permute-start | bytes 3440648 | tf_op jit(solution)/shard_map/cond/branch_1_fun/ppermute | solution.py:415
  17.1 27.8 %collective-permute-start.24 = (bf16[2,7,2,160,128]{4,3,2,1,0:T(8,128)(2,1)S(1)}, bf16[2,7,2,160,128]{4,3,2,1,0:T(8,128)(2,1)S(1)}, u32[]{:S(2)}, u32[]{:S(2)}) collective-permute-start(bf16[2,7,2,160,128]{4,3,2,1,0:T(8,128)(2,1)S(1)} %get-tuple-element.89), channel_id=1, source_target_pairs={{1,2},{3,4},{5,6},{2,1},{4,3},{6,5},{9,10},{11,12},{13,14},{10,9},... | collective-permute-start | bytes 3440648 | tf_op jit(solution)/shard_map/cond/branch_1_fun/ppermute | solution.py:421
  24.6 22.3 %collective-permute-start.26 = (bf16[2,6,2,160,128]{4,3,2,1,0:T(8,128)(2,1)S(1)}, bf16[2,6,2,160,128]{4,3,2,1,0:T(8,128)(2,1)S(1)}, u32[]{:S(2)}, u32[]{:S(2)}) collective-permute-start(bf16[2,6,2,160,128]{4,3,2,1,0:T(8,128)(2,1)S(1)} %collective-permute-done.25.refs_1_), channel_id=1, source_target_pairs={{7,4},{0,3},{15,12},{8,11},{23,20},{16,19},{31,28},{24,27}} | collective-permute-start | bytes 2949128 | tf_op jit(solution)/shard_map/cond/branch_1_fun/ppermute | solution.py:590
  46.9 11.7 %copy-start.5 = (bf16[2,1,160,2560]{3,2,1,0:T(8,128)(2,1)S(1)}, bf16[2,1,160,2560]{3,2,1,0:T(8,128)(2,1)}, u32[]{:S(2)}) copy-start(bf16[2,1,160,2560]{3,2,1,0:T(8,128)(2,1)} %get-tuple-element.86.q_ref) | copy-start | bytes 4915204 | tf_op jit(solution)/shard_map/cond
  46.9 37.7 %collective-permute-start.33 = (bf16[320,2560]{1,0:T(8,128)(2,1)S(1)}, bf16[320,2560]{1,0:T(8,128)(2,1)S(1)}, u32[]{:S(2)}, u32[]{:S(2)}) collective-permute-start(bf16[320,2560]{1,0:T(8,128)(2,1)S(1)} %copy-done.13), channel_id=1, source_target_pairs={{0,2},{1,3},{2,0},{3,1},{4,6},{5,7},{6,4},{7,5},{8,10},{9,11},{10,... | collective-permute-start | bytes 4915208 | tf_op jit(solution)/shard_map/cond/branch_1_fun/ppermute | solution.py:431
  49.3 39.3 %collective-permute-start.34 = (bf16[320,2560]{1,0:T(8,128)(2,1)S(1)}, bf16[320,2560]{1,0:T(8,128)(2,1)S(1)}, u32[]{:S(2)}, u32[]{:S(2)}) collective-permute-start(bf16[320,2560]{1,0:T(8,128)(2,1)S(1)} %copy-done.13), channel_id=1, source_target_pairs={{0,4},{1,5},{2,6},{3,7},{4,0},{5,1},{6,2},{7,3},{8,12},{9,13},{10,... | collective-permute-start | bytes 4915208 | tf_op jit(solution)/shard_map/cond/branch_1_fun/ppermute | solution.py:431
  53.6 24.1 %collective-permute-start.32 = (bf16[2,9,2,160,128]{4,3,2,1,0:T(8,128)(2,1)S(1)}, bf16[2,9,2,160,128]{4,3,2,1,0:T(8,128)(2,1)S(1)}, u32[]{:S(2)}, u32[]{:S(2)}) collective-permute-start(bf16[2,9,2,160,128]{4,3,2,1,0:T(8,128)(2,1)S(1)} %get-tuple-element.110), channel_id=1, source_target_pairs={{0,1},{1,0},{2,3},{3,2},{4,5},{5,4},{6,7},{7,6},{8,9},{9,8},{10,11... | collective-permute-start | bytes 4423688 | tf_op jit(solution)/shard_map/cond/branch_1_fun/ppermute | solution.py:431
  53.7 22.5 %collective-permute-start.30 = (bf16[9,2,160,128]{3,2,1,0:T(8,128)(2,1)S(1)}, bf16[9,2,160,128]{3,2,1,0:T(8,128)(2,1)S(1)}, u32[]{:S(2)}, u32[]{:S(2)}) collective-permute-start(bf16[9,2,160,128]{3,2,1,0:T(8,128)(2,1)S(1)} %get-tuple-element.108), channel_id=1, source_target_pairs={{0,8},{8,16},{16,24},{1,9},{9,17},{17,25},{2,10},{10,18},{18,26},{... | collective-permute-start | bytes 2211848 | tf_op jit(solution)/shard_map/cond/branch_1_fun/ppermute | solution.py:415
  57.2 20.5 %collective-permute-start.31 = (bf16[9,2,160,128]{3,2,1,0:T(8,128)(2,1)S(1)}, bf16[9,2,160,128]{3,2,1,0:T(8,128)(2,1)S(1)}, u32[]{:S(2)}, u32[]{:S(2)}) collective-permute-start(bf16[9,2,160,128]{3,2,1,0:T(8,128)(2,1)S(1)} %get-tuple-element.109), channel_id=1, source_target_pairs={{8,0},{16,8},{24,16},{9,1},{17,9},{25,17},{10,2},{18,10},{26,18},{... | collective-permute-start | bytes 2211848 | tf_op jit(solution)/shard_map/cond/branch_1_fun/ppermute | solution.py:415
  76.2 12.5 %copy-start.11 = (bf16[2560,64]{0,1:T(8,128)(2,1)S(1)}, bf16[2560,64]{0,1:T(8,128)(2,1)}, u32[]{:S(2)}) copy-start(bf16[2560,64]{0,1:T(8,128)(2,1)} %get-tuple-element.122) | copy-start | bytes 983044 | tf_op jit(solution)/shard_map/cond
  90.2 2.2 %collective-permute-start.35 = (f32[64,2560]{1,0:T(8,128)S(1)}, f32[64,2560]{1,0:T(8,128)S(1)}, u32[]{:S(2)}, u32[]{:S(2)}) collective-permute-start(f32[64,2560]{1,0:T(8,128)S(1)} %get-tuple-element.190), channel_id=1, source_target_pairs={{0,1},{1,0},{2,3},{3,2},{4,5},{5,4},{6,7},{7,6},{8,9},{9,8},{10,11... | collective-permute-start | bytes 1966088 | tf_op jit(solution)/shard_map/cond/branch_1_fun/ppermute | solution.py:431
  92.5 6.3 %collective-permute-start.36 = (bf16[32,2560]{1,0:T(8,128)(2,1)S(1)}, bf16[32,2560]{1,0:T(8,128)(2,1)S(1)}, u32[]{:S(2)}, u32[]{:S(2)}) collective-permute-start(bf16[32,2560]{1,0:T(8,128)(2,1)S(1)} %select_convert_fusion.2), channel_id=1, source_target_pairs={{0,2},{1,3},{2,0},{3,1},{4,6},{5,7},{6,4},{7,5},{8,10},{9,11},{10,... | collective-permute-start | bytes 491528 | tf_op jit(solution)/shard_map/cond/branch_1_fun/ppermute | solution.py:431
  98.9 4.5 %collective-permute-start.37 = (bf16[16,2560]{1,0:T(8,128)(2,1)S(1)}, bf16[16,2560]{1,0:T(8,128)(2,1)S(1)}, u32[]{:S(2)}, u32[]{:S(2)}) collective-permute-start(bf16[16,2560]{1,0:T(8,128)(2,1)S(1)} %select_convert_fusion.3), channel_id=1, source_target_pairs={{0,4},{1,5},{2,6},{3,7},{4,0},{5,1},{6,2},{7,3},{8,12},{9,13},{10,... | collective-permute-start | bytes 245768 | tf_op jit(solution)/shard_map/cond/branch_1_fun/ppermute | solution.py:431
  99.2 16.0 %collective-permute-start.42 = (bf16[320,2560]{1,0:T(8,128)(2,1)S(1)}, bf16[320,2560]{1,0:T(8,128)(2,1)S(1)}, u32[]{:S(2)}, u32[]{:S(2)}) collective-permute-start(bf16[320,2560]{1,0:T(8,128)(2,1)S(1)} %collective-permute-done.33.odd_ref.refs_2_), channel_id=1, source_target_pairs={{0,1},{1,0},{2,3},{3,2},{4,5},{5,4},{6,7},{7,6},{8,9},{9,8},{10,11... | collective-permute-start | bytes 4915208 | tf_op jit(solution)/shard_map/cond/branch_1_fun/ppermute | solution.py:431
  99.2 16.1 %collective-permute-start.43 = (bf16[320,2560]{1,0:T(8,128)(2,1)S(1)}, bf16[320,2560]{1,0:T(8,128)(2,1)S(1)}, u32[]{:S(2)}, u32[]{:S(2)}) collective-permute-start(bf16[320,2560]{1,0:T(8,128)(2,1)S(1)} %collective-permute-done.34.even_ref.refs_4_), channel_id=1, source_target_pairs={{0,1},{1,0},{2,3},{3,2},{4,5},{5,4},{6,7},{7,6},{8,9},{9,8},{10,11... | collective-permute-start | bytes 4915208 | tf_op jit(solution)/shard_map/cond/branch_1_fun/ppermute | solution.py:431
  100.4 14.9 %collective-permute-start.41 = (bf16[320,2560]{1,0:T(8,128)(2,1)S(1)}, bf16[320,2560]{1,0:T(8,128)(2,1)S(1)}, u32[]{:S(2)}, u32[]{:S(2)}) collective-permute-start(bf16[320,2560]{1,0:T(8,128)(2,1)S(1)} %copy-done.13), channel_id=1, source_target_pairs={{0,1},{1,0},{2,3},{3,2},{4,5},{5,4},{6,7},{7,6},{8,9},{9,8},{10,11... | collective-permute-start | bytes 4915208 | tf_op jit(solution)/shard_map/cond/branch_1_fun/ppermute | solution.py:431
  103.4 4.7 %collective-permute-start.38 = (bf16[16,2560]{1,0:T(8,128)(2,1)S(1)}, bf16[16,2560]{1,0:T(8,128)(2,1)S(1)}, u32[]{:S(2)}, u32[]{:S(2)}) collective-permute-start(bf16[16,2560]{1,0:T(8,128)(2,1)S(1)} %convert_add_fusion.3), channel_id=1, source_target_pairs={{0,8},{8,0},{16,24},{24,16},{1,9},{9,1},{17,25},{25,17},{2,10},{10... | collective-permute-start | bytes 245768 | tf_op jit(solution)/shard_map/cond/branch_1_fun/ppermute | solution.py:431
  105.7 21.1 %collective-permute-start.40 = (bf16[320,2560]{1,0:T(8,128)(2,1)S(1)}, bf16[320,2560]{1,0:T(8,128)(2,1)S(1)}, u32[]{:S(2)}, u32[]{:S(2)}) collective-permute-start(bf16[320,2560]{1,0:T(8,128)(2,1)S(1)} %choose_by_kind.3), channel_id=1, source_target_pairs={{0,2},{1,5},{2,0},{3,7},{4,6},{5,1},{6,4},{7,3},{8,10},{9,13},{10,... | collective-permute-start | bytes 4915208 | tf_op jit(solution)/shard_map/cond/branch_1_fun/ppermute | solution.py:427
  108.1 7.1 %collective-permute-start.39 = (bf16[16,2560]{1,0:T(8,128)(2,1)S(1)}, bf16[16,2560]{1,0:T(8,128)(2,1)S(1)}, u32[]{:S(2)}, u32[]{:S(2)}) collective-permute-start(bf16[16,2560]{1,0:T(8,128)(2,1)S(1)} %add_convert_fusion.3), channel_id=1, source_target_pairs={{0,16},{8,24},{16,0},{24,8},{1,17},{9,25},{17,1},{25,9},{2,18},{10... | collective-permute-start | bytes 245768 | tf_op jit(solution)/shard_map/cond/branch_1_fun/ppermute | solution.py:431
  126.8 4.4 %collective-permute-start.44 = (bf16[16,2560]{1,0:T(8,128)(2,1)S(1)}, bf16[16,2560]{1,0:T(8,128)(2,1)S(1)}, u32[]{:S(2)}, u32[]{:S(2)}) collective-permute-start(bf16[16,2560]{1,0:T(8,128)(2,1)S(1)} %add_convert_fusion.2), channel_id=1, source_target_pairs={{0,4},{1,5},{2,6},{3,7},{4,0},{5,1},{6,2},{7,3},{8,12},{9,13},{10,... | collective-permute-start | bytes 245768 | tf_op jit(solution)/shard_map/cond/branch_1_fun/ppermute | solution.py:431
  127.2 9.5 %collective-permute-start.46 = (bf16[320,2560]{1,0:T(8,128)(2,1)S(1)}, bf16[320,2560]{1,0:T(8,128)(2,1)S(1)}, u32[]{:S(2)}, u32[]{:S(2)}) collective-permute-start(bf16[320,2560]{1,0:T(8,128)(2,1)S(1)} %collective-permute-done.40.refs_0_), channel_id=1, source_target_pairs={{0,1},{1,0},{2,3},{3,2},{4,5},{5,4},{6,7},{7,6},{8,9},{9,8},{10,11... | collective-permute-start | bytes 4915208 | tf_op jit(solution)/shard_map/cond/branch_1_fun/ppermute | solution.py:431
  131.3 5.4 %collective-permute-start.45 = (bf16[32,2560]{1,0:T(8,128)(2,1)S(1)}, bf16[32,2560]{1,0:T(8,128)(2,1)S(1)}, u32[]{:S(2)}, u32[]{:S(2)}) collective-permute-start(bf16[32,2560]{1,0:T(8,128)(2,1)S(1)} %pad_maximum_fusion.3), channel_id=1, source_target_pairs={{0,2},{1,3},{2,0},{3,1},{4,6},{5,7},{6,4},{7,5},{8,10},{9,11},{10,... | collective-permute-start | bytes 491528 | tf_op jit(solution)/shard_map/cond/branch_1_fun/ppermute | solution.py:431
  136.8 5.1 %collective-permute-start.47 = (bf16[64,2560]{1,0:T(8,128)(2,1)S(1)}, bf16[64,2560]{1,0:T(8,128)(2,1)S(1)}, u32[]{:S(2)}, u32[]{:S(2)}) collective-permute-start(bf16[64,2560]{1,0:T(8,128)(2,1)S(1)} %pad_maximum_fusion.2), channel_id=1, source_target_pairs={{0,1},{1,0},{2,3},{3,2},{4,5},{5,4},{6,7},{7,6},{8,9},{9,8},{10,11... | collective-permute-start | bytes 983048 | tf_op jit(solution)/shard_map/cond/branch_1_fun/ppermute | solution.py:431
  142.2 1.6 %copy-start.16 = (bf16[2,1,160,2560]{3,2,0,1:T(8,128)(2,1)}, bf16[2,1,160,2560]{3,2,0,1:T(8,128)(2,1)S(1)}, u32[]{:S(2)}) copy-start(bf16[2,1,160,2560]{3,2,0,1:T(8,128)(2,1)S(1)} %get-tuple-element.162) | copy-start | bytes 4915204
  (2 other events, 1.9 us)
